TPU v7x, 256 devices: a whole 4x4x8 slice. The times are simulated.
256 devices in a mesh: batch: 32 (over x, z), node: 4 (over y), replica: 2 (over core).
Axes of the slice: x: 4, y: 4, z: 8, core: 2. Of those that a mesh axis runs over, the one named last changes fastest.
Arguments:
- embed_table: bfloat16 [32768, 1024], P('batch'), may hold values from -6 to 6
- owner_shard: int32 [64, 256, 1], P(('batch', 'replica')), may hold values from 0 to 31; in each aligned block of 256 rows (0 to 255, 256 to 511, ..., all dimensions but the last counted through in order) at most 12 rows name the same one
- local_row: int32 [64, 256], P(('batch', 'replica')), may hold values from 0 to 1023
- lengths: int32 [64], P(('batch', 'replica')), may hold values from 64 to 256
- spd_bucket: int32 [64, 256, 256], P(('batch', 'replica')), may hold values from 0 to 15, as said below
- degree_bucket: int32 [64, 256], P(('batch', 'replica')), may hold values from 0 to 31, as said below
- w_query: bfloat16 [1024, 1024], P(None, 'node'), may hold values from -0.1875 to 0.1875
- w_key: bfloat16 [1024, 1024], P(None, 'node'), may hold values from -0.1875 to 0.1875
- w_value: bfloat16 [1024, 1024], P(None, 'node'), may hold values from -0.1875 to 0.1875
- w_out: bfloat16 [1024, 1024], P('node'), may hold values from -0.1875 to 0.1875
- spd_bias: float32 [16, 16], P(None, 'node'), may hold values from -4 to 4
- degree_bias: float32 [32, 16], P(None, 'node'), may hold values from -2 to 253
- cotangent: bfloat16 [64, 256, 1024], P(('batch', 'replica')), may hold values from -6 to 6
Outputs:
- table_grad: float32 [32768, 1024], P('batch', ('node', 'replica'))
- query_grad: float32 [1024, 1024], P(None, 'node')
- key_grad: float32 [1024, 1024], P(None, 'node')
- value_grad: float32 [1024, 1024], P(None, 'node')
- out_grad: float32 [1024, 1024], P('node')
- spd_grad: float32 [16, 16], P(None, 'node')
- degree_grad: float32 [32, 16], P(None, 'node')
Inputs may be any that keep to these rules, and one draw needn't show every extreme that they name: `owner_shard`: in each aligned block of 256 slots (the subgraphs of one index of batch and replica) no owner shard is named by more than 12 slots, a bound that some block reaches. `lengths`: slots at or past a subgraph's length are padding. `spd_bucket`: symmetric in its last two dimensions, 0 exactly on the diagonal. `degree_bucket`: some subgraphs hold only buckets below half of 32.
All inputs are finite; a program needn't handle non-finite values.
Results may differ from a plain program's by a relative error of at most 0.015.
Values may be sent and summed in bfloat16 or wider, within the bound.
A program may use at most 64 MiB of HBM per device.

v0:
```python
import jax
import jax.numpy as jnp
from jax import lax
from jax.sharding import PartitionSpec as P

HEAD_DIM = 64
NSPD = 16
NDEG = 32
EPS = 1e-05


def normalize(rows_in):
    widened = rows_in.astype(jnp.float32)
    mean_val = jnp.mean(widened, axis=-1, keepdims=True)
    centred = widened - mean_val
    inv_std = lax.rsqrt(jnp.mean(centred * centred, axis=-1, keepdims=True) + EPS)
    return (centred * inv_std, inv_std)


def on_device(
    embed_table,
    owner_shard,
    local_row,
    lengths,
    spd_bucket,
    degree_bucket,
    w_query,
    w_key,
    w_value,
    w_out,
    spd_bias,
    degree_bias,
    cotangent,
):
    group_count, slot_count, feature_dim = cotangent.shape
    slot_total = group_count * slot_count
    row_count = embed_table.shape[0]
    peer_count = lax.axis_size("batch")
    capacity = 3 * slot_total // (2 * peer_count)
    dest_shard = owner_shard.reshape(slot_total)
    wanted = local_row.reshape(slot_total)
    bucket_hits = (dest_shard[:, None] == jnp.arange(peer_count, dtype=jnp.int32)[None, :]).astype(
        jnp.int32
    )
    bucket_rank = jnp.sum((jnp.cumsum(bucket_hits, axis=0) - bucket_hits) * bucket_hits, axis=1)
    slot_place = dest_shard * capacity + bucket_rank
    requests = jnp.full((peer_count * capacity,), -1, jnp.int32).at[slot_place].set(wanted)
    asked_rows = lax.all_to_all(
        requests.reshape(peer_count, capacity), "batch", split_axis=0, concat_axis=0, tiled=True
    ).reshape(peer_count * capacity)
    present = asked_rows >= 0
    safe_rows = jnp.where(present, asked_rows, 0)
    target_rows = jnp.where(present, asked_rows, row_count)
    fetched = lax.all_to_all(
        embed_table[safe_rows].reshape(peer_count, capacity, feature_dim),
        "batch",
        split_axis=0,
        concat_axis=0,
        tiled=True,
    )
    slot_rows = fetched.reshape(peer_count * capacity, feature_dim)[slot_place]
    x_hat, inv_std = normalize(slot_rows)
    normed = x_hat.astype(jnp.bfloat16)
    local_width = w_query.shape[1]
    head_local = local_width // HEAD_DIM
    head_shape = (group_count, slot_count, head_local, HEAD_DIM)
    score_scale = HEAD_DIM ** (-0.5)

    def project(weight):
        return jnp.dot(normed, weight, preferred_element_type=jnp.float32).astype(jnp.bfloat16)

    queries = project(w_query).reshape(head_shape)
    key_rows = project(w_key).reshape(head_shape)
    values = project(w_value).reshape(head_shape)
    valid_slot = jnp.arange(slot_count, dtype=jnp.int32)[None, :] < lengths[:, None]
    spd_hot = (spd_bucket[..., None] == jnp.arange(NSPD, dtype=jnp.int32)).astype(jnp.float32)
    degree_hot = (degree_bucket[..., None] == jnp.arange(NDEG, dtype=jnp.int32)).astype(jnp.float32)
    spd_term = jnp.einsum("gijb,bh->ghij", spd_hot, spd_bias, precision=lax.Precision.HIGHEST)
    degree_term = jnp.einsum(
        "gjb,bh->ghj", degree_hot, degree_bias, precision=lax.Precision.HIGHEST
    )[:, :, None, :]
    scores = (
        jnp.einsum("gihd,gjhd->ghij", queries, key_rows, preferred_element_type=jnp.float32)
        * score_scale
        + spd_term
        + degree_term
    )
    scores = jnp.where(valid_slot[:, None, None, :], scores, -jnp.inf)
    row_top = jnp.max(scores, axis=-1, keepdims=True)
    exp_scores = jnp.exp(scores - row_top)
    probs = exp_scores / jnp.sum(exp_scores, axis=-1, keepdims=True)
    probs_b = probs.astype(jnp.bfloat16)
    attended = (
        jnp.einsum("ghij,gjhd->gihd", probs_b, values, preferred_element_type=jnp.float32)
        .astype(jnp.bfloat16)
        .reshape(slot_total, local_width)
    )
    d_masked = jnp.where(valid_slot[:, :, None], cotangent, jnp.zeros_like(cotangent)).reshape(
        slot_total, feature_dim
    )
    d_att = jnp.dot(d_masked, w_out.T, preferred_element_type=jnp.float32).astype(jnp.bfloat16)
    out_part = jnp.dot(attended.T, d_masked, preferred_element_type=jnp.float32)
    d_att_h = d_att.reshape(head_shape)
    d_values = (
        jnp.einsum("ghij,gihd->gjhd", probs_b, d_att_h, preferred_element_type=jnp.float32)
        .astype(jnp.bfloat16)
        .reshape(slot_total, local_width)
    )
    d_probs = jnp.einsum("gihd,gjhd->ghij", d_att_h, values, preferred_element_type=jnp.float32)
    d_scores = probs * (d_probs - jnp.sum(probs * d_probs, axis=-1, keepdims=True))
    spd_part = jnp.einsum("gijb,ghij->bh", spd_hot, d_scores, precision=lax.Precision.HIGHEST)
    degree_part = jnp.einsum("gjb,ghij->bh", degree_hot, d_scores, precision=lax.Precision.HIGHEST)
    d_scores_b = d_scores.astype(jnp.bfloat16)
    d_queries = (
        (
            jnp.einsum("ghij,gjhd->gihd", d_scores_b, key_rows, preferred_element_type=jnp.float32)
            * score_scale
        )
        .astype(jnp.bfloat16)
        .reshape(slot_total, local_width)
    )
    d_keys = (
        (
            jnp.einsum("ghij,gihd->gjhd", d_scores_b, queries, preferred_element_type=jnp.float32)
            * score_scale
        )
        .astype(jnp.bfloat16)
        .reshape(slot_total, local_width)
    )
    query_part = jnp.dot(normed.T, d_queries, preferred_element_type=jnp.float32)
    key_part = jnp.dot(normed.T, d_keys, preferred_element_type=jnp.float32)
    value_part = jnp.dot(normed.T, d_values, preferred_element_type=jnp.float32)
    d_normed = (
        jnp.dot(d_queries, w_query.T, preferred_element_type=jnp.float32)
        + jnp.dot(d_keys, w_key.T, preferred_element_type=jnp.float32)
        + jnp.dot(d_values, w_value.T, preferred_element_type=jnp.float32)
    )
    lead_flag = (lax.axis_index("node") == 0).astype(jnp.float32)
    d_rows = lead_flag * d_masked.astype(jnp.float32) + inv_std * (
        d_normed
        - jnp.mean(d_normed, axis=-1, keepdims=True)
        - x_hat * jnp.mean(d_normed * x_hat, axis=-1, keepdims=True)
    )
    send_back = (
        jnp.zeros((peer_count * capacity, feature_dim), jnp.float32).at[slot_place].set(d_rows)
    )
    returned = (
        lax.all_to_all(
            send_back.reshape(peer_count, capacity, feature_dim).astype(jnp.bfloat16),
            "batch",
            split_axis=0,
            concat_axis=0,
            tiled=True,
        )
        .astype(jnp.float32)
        .reshape(peer_count * capacity, feature_dim)
    )
    accum = (
        jnp.zeros((row_count, feature_dim), jnp.float32).at[target_rows].add(returned, mode="drop")
    )
    table_grad = lax.psum_scatter(
        accum.astype(jnp.bfloat16), ("node", "replica"), scatter_dimension=1, tiled=True
    ).astype(jnp.float32)
    summed = lax.psum(
        (query_part, key_part, value_part, out_part, spd_part, degree_part), ("batch", "replica")
    )
    copies = float(peer_count * lax.axis_size("replica"))
    return (
        table_grad,
        summed[0] / copies,
        summed[1] / copies,
        summed[2] / copies,
        summed[3] / copies,
        summed[4] / copies,
        summed[5] / copies,
    )


def solution(mesh):
    placed = (
        P("batch", None),
        P(("batch", "replica"), None, None),
        P(("batch", "replica"), None),
        P(("batch", "replica")),
        P(("batch", "replica"), None, None),
        P(("batch", "replica"), None),
        P(None, "node"),
        P(None, "node"),
        P(None, "node"),
        P("node", None),
        P(None, "node"),
        P(None, "node"),
        P(("batch", "replica"), None, None),
    )
    return jax.shard_map(
        on_device,
        mesh=mesh,
        in_specs=placed,
        out_specs=(
            P("batch", ("node", "replica")),
            P(None, "node"),
            P(None, "node"),
            P(None, "node"),
            P("node", None),
            P(None, "node"),
            P(None, "node"),
        ),
        check_vma=False,
    )
```

profile of v0, /device:TPU:8, one launch (start us, length us, event | category | flops | bytes accessed | tf_op | source)
XLA Modules:
  0.0 310.1 jit_solution(10417535351380792851)
XLA Ops:
  8.0 0.8 fusion.50
  8.8 0.6 reduce-window.6
  9.4 0.2 slice_reduce_fusion
  9.7 0.8 fusion.49
  10.4 0.7 compare_select_fusion.4
  11.1 1.6 scatter_custom_fusion
  12.8 20.9 %all_to_all.19 = s32[32,1,12]{2,1,0:T(1,128)S(1)} all-to-all(s32[32,1,12]{2,1,0:T(1,128)S(1)} %bitcast.120), channel_id=1, replica_groups=mesh['batch'=32,'node'=4,'replica'=2] {'batch'}, dimensions={0} | all-to-all | bytes 3072 | tf_op jit(solution)/shard_map/all_to_all | solution.py:48
  33.7 0.5 broadcast.245
  34.2 0.7 reduce.17
  34.9 0.1 reshape.325
  35.0 0.6 fusion.53
  35.6 2.1 gather_fusion
  37.7 1.1 reshape.327
  38.9 4.7 %all-to-all-start.1 = ((bf16[32,12,1024]{2,1,0:T(8,128)(2,1)}), bf16[32,12,1024]{2,1,0:T(8,128)(2,1)}, u32[]{:S(2)}, u32[]{:S(2)}) async-start(bf16[32,12,1024]{2,1,0:T(8,128)(2,1)} %reshape.327), calls=%async_computation.1 | async-start | bytes 2097152 | tf_op jit(solution)/shard_map/all_to_all | solution.py:54
  43.6 1.3 fusion.2
  44.9 1.4 copy.39
  47.0 0.2 convolution_bitcast_fusion
  47.2 2.3 convolution_convert_fusion.3
  49.5 21.5 %all-to-all-done.1 = bf16[32,12,1024]{2,1,0:T(8,128)(2,1)} async-done(((bf16[32,12,1024]{2,1,0:T(8,128)(2,1)}), bf16[32,12,1024]{2,1,0:T(8,128)(2,1)}, u32[]{:S(2)}, u32[]{:S(2)}) %all-to-all-start.1) | async-done | bytes 786464 | tf_op jit(solution)/shard_map/all_to_all | solution.py:54
  71.1 1.3 reshape.328
  72.4 1.2 gather_fusion.1
  73.6 0.1 convert_reduce_fusion
  73.7 0.3 fusion.26
  74.0 1.5 convolution_convert_fusion.5
  75.5 0.5 convolution_convert_fusion.4
  76.0 0.4 fusion.11
  76.4 0.8 fusion.67
  77.2 0.5 convolution_convert_fusion.2
  77.7 0.4 multiply_reduce_fusion
  78.1 0.2 fusion.66
  78.3 0.2 fusion.17
  78.5 0.8 copy-done.1
  79.3 0.3 fusion.18
  79.5 1.9 convolution_convert_fusion.1
  81.5 2.4 fusion.68
  83.9 1.4 fusion.60
  85.3 1.9 convolution_convert_fusion
  87.3 1.5 fusion.58
  88.7 1.5 fusion.56
  90.2 1.4 fusion.31
  91.6 0.2 reduce-scatter.4.cloned.1.call-start
  91.8 1.8 convolution_add_fusion.1
  93.6 1.4 fusion.65
  95.0 3.8 %scatter_custom_fusion.1 = f32[384,1024]{1,0:T(8,128)} fusion(s32[256]{0:T(256)} %bitcast.125, bf16[256,1024]{1,0:T(8,128)(2,1)S(1)} %gather_fusion.1, f32[256,1024]{1,0:T(8,128)} %get-tuple-element.23, f32[]{:T(128)} %constant.15.clone.1, f32[256]{0:T(256)S(1)} %get-tuple-element.24, f32[256]{0:T(256)S(1)} %get-tuple-element.25, ...), kind=kCustom, calls=%fused_computation.44 | custom fusion | flops 2883584 | bytes 3674884 | tf_op jit(solution)/shard_map/scatter | solution.py:145
  98.8 2.5 convert_element_type.111
  101.3 1.2 convert_element_type.112
  102.5 35.3 %all_to_all.20 = bf16[32,12,1024]{2,1,0:T(8,128)(2,1)} all-to-all(bf16[32,12,1024]{2,1,0:T(8,128)(2,1)S(1)} %convert_element_type.112), channel_id=1, replica_groups=mesh['batch'=32,'node'=4,'replica'=2] {'batch'}, dimensions={0} | all-to-all | bytes 1572864 | tf_op jit(solution)/shard_map/all_to_all | solution.py:148
  137.9 2.4 reshape.377
  140.2 6.6 %scatter_custom_fusion.2 = f32[1024,1024]{1,0:T(8,128)} fusion(s32[384]{0:T(512)} %get-tuple-element.10, f32[384,1024]{1,0:T(8,128)} %reshape.377, f32[]{:T(128)} %constant.15.clone.1), kind=kCustom, calls=%fused_computation.11 | custom fusion | flops 393216 | bytes 4194816 | tf_op jit(solution)/shard_map/scatter-add | solution.py:159
  146.9 3.9 %convert_element_type.113 = bf16[1024,1024]{1,0:T(8,128)(2,1)} convert(f32[1024,1024]{1,0:T(8,128)} %scatter_custom_fusion.2) | non-fusion elementwise | flops 1048576 | bytes 6291456 | tf_op jit(solution)/shard_map/convert_element_type | solution.py:162
  150.8 4.0 %copy.52 = bf16[1024,1024]{0,1:T(8,128)(2,1)} copy(bf16[1024,1024]{1,0:T(8,128)(2,1)} %convert_element_type.113) | data formatting | bytes 4194304
  154.8 1.2 copy-done.2
  156.0 1.3 copy.46
  157.3 4.0 %fusion.19 = f32[16,4]{0,1:T(4,128)S(1)} fusion(f32[4,256,256]{2,0,1:T(4,128)} %copy.46, s32[256,256]{1,0:T(8,128)S(1)} %bitcast.117), kind=kOutput, calls=%fused_computation.39 | convolution fusion | flops 51380224 | bytes 1310976 | tf_op jit(solution)/shard_map/gijb,ghij->bh/dot_general | solution.py:111
  161.2 0.2 fusion.44
  161.5 127.4 %all-reduce = (f32[16,4]{0,1:T(4,128)S(1)}, f32[32,4]{0,1:T(4,128)S(1)}) all-reduce(f32[16,4]{0,1:T(4,128)S(1)} %fusion.19, f32[32,4]{0,1:T(4,128)S(1)} %fusion.44), channel_id=1, replica_groups=mesh['batch'=32,'node'=4,'replica'=2] {'batch','replica'}, use_global_device_ids=true, to_apply=%region_18.19 | all-reduce | flops 192 | bytes 1536 | tf_op jit(solution)/shard_map/psum | solution.py:164
  288.9 0.6 broadcast_multiply_fusion.5
  289.5 0.6 broadcast_multiply_fusion.4
  290.0 5.7 %all-reduce.4.cloned.1.call-done = (f32[1024,256]{1,0:T(8,128)}, f32[1024,256]{1,0:T(8,128)}, f32[1024,256]{1,0:T(8,128)}, f32[256,1024]{1,0:T(8,128)}) async-done(((f32[1024,256]{1,0:T(8,128)}, f32[1024,256]{1,0:T(8,128)}, f32[1024,256]{1,0:T(8,128)}, f32[256,1024]{1,0:T(8,128)}), (f32[1024,256]{1,0:T(8,128)}, f32[1024,256]{1,0:T(8,128)}, f32[1024,256]{1,0:T(8,128)}, ...) | async-done | bytes 4194320 | tf_op jit(solution)/shard_map/psum | solution.py:164
  295.7 2.4 broadcast_multiply_fusion.3
  298.1 1.1 broadcast_multiply_fusion
  299.2 1.5 broadcast_multiply_fusion.1
  300.7 1.1 copy.53
  301.8 0.8 convert_element_type.114
  (51 shorter events, 0.4 us)
Async XLA Ops:
  8.0 27.6 %copy-start = (bf16[1024,1024]{1,0:T(8,128)(2,1)S(1)}, bf16[1024,1024]{1,0:T(8,128)(2,1)}, u32[]{:S(2)}) copy-start(bf16[1024,1024]{1,0:T(8,128)(2,1)} %param.13) | copy-start | bytes 6291460
  11.1 35.8 %copy-start.14 = (s32[256,1]{0,1:T(1,128)}, s32[256,1]{0,1:T(1,128)S(1)}, u32[]{:S(2)}) copy-start(s32[256,1]{0,1:T(1,128)S(1)} %compare_select_fusion.4) | copy-start | bytes 3076
  37.7 5.9 %copy-start.12 = (s32[1,256,256]{2,1,0:T(8,128)S(1)}, s32[1,256,256]{2,1,0:T(8,128)}, u32[]{:S(2)}) copy-start(s32[1,256,256]{2,1,0:T(8,128)} %param.17) | copy-start | bytes 786436
  37.7 5.9 %copy-start.15 = (f32[16,4]{0,1:T(4,128)S(1)}, f32[16,4]{0,1:T(4,128)}, u32[]{:S(2)}) copy-start(f32[16,4]{0,1:T(4,128)} %param.23) | copy-start | bytes 772
  38.9 32.2 %all-to-all-start.1 = ((bf16[32,12,1024]{2,1,0:T(8,128)(2,1)}), bf16[32,12,1024]{2,1,0:T(8,128)(2,1)}, u32[]{:S(2)}, u32[]{:S(2)}) async-start(bf16[32,12,1024]{2,1,0:T(8,128)(2,1)} %reshape.327), calls=%async_computation.1 | async-start | bytes 2097152 | tf_op jit(solution)/shard_map/all_to_all | solution.py:54
  43.5 3.4 %copy-start.16 = (f32[32,4]{0,1:T(4,128)S(1)}, f32[32,4]{0,1:T(4,128)}, u32[]{:S(2)}) copy-start(f32[32,4]{0,1:T(4,128)} %param.24) | copy-start | bytes 1540
  43.5 3.4 %copy-start.17 = (s32[1,256]{1,0:T(1,128)S(1)}, s32[1,256]{1,0:T(1,128)}, u32[]{:S(2)}) copy-start(s32[1,256]{1,0:T(1,128)} %param.18) | copy-start | bytes 3076
  43.5 252.2 %all-reduce.4.cloned.1.call-start = ((), (), s32[]{:S(2)}) async-start(), calls=%async_computation.5 | async-start | bytes 8388608 | tf_op jit(solution)/shard_map/psum | solution.py:164
  73.6 2.0 copy-start.11
  73.6 2.4 copy-start.3
  76.0 1.2 copy-start.9
  76.4 1.6 copy-start.4
  76.4 1.3 copy-start.19
  78.3 1.0 copy-start.1
  87.3 2.9 copy-start.5
  91.6 209.1 %reduce-scatter.4.cloned.1.call-start = ((), (), s32[]{:S(2)}) async-start(), calls=%async_computation.4 | async-start | bytes 2359296
  91.8 1.8 copy-start.10
  154.7 1.2 copy-start.2
  154.7 2.5 copy-start.13
  156.0 5.3 %copy-start.18 = (s32[1,256]{1,0:T(1,128)S(1)}, s32[1,256]{1,0:T(1,128)}, u32[]{:S(2)}) copy-start(s32[1,256]{1,0:T(1,128)} %param.18) | copy-start | bytes 3076
  295.7 2.4 copy-start.6
  295.7 3.5 %copy-start.7 = (f32[1024,256]{1,0:T(8,128)S(1)}, f32[1024,256]{1,0:T(8,128)}, u32[]{:S(2)}) copy-start(f32[1024,256]{1,0:T(8,128)} %get-tuple-element.14) | copy-start | bytes 3145732
  295.7 3.5 %copy-start.8 = (f32[1024,256]{1,0:T(8,128)S(1)}, f32[1024,256]{1,0:T(8,128)}, u32[]{:S(2)}) copy-start(f32[1024,256]{1,0:T(8,128)} %get-tuple-element.15) | copy-start | bytes 3145732
Sparse Core Ops, SparseCore 0:
  91.7 203.9 all-reduce.3
Sparse Core Ops, SparseCore 1:
  154.8 32.6 reduce-scatter.3
where the time goes:
time: 311 us; the launch traced here: 310 us
  blocking collectives  184 us (59%)
  other arithmetic  29.4 us (9%)
  waiting for transfers between devices  27.2 us (9%)
  matrix products  26.8 us (9%)
  local copies, waits for them, and re-layouts  21.6 us (7%)
  between operations  16.5 us (5%)
  starting transfers between devices  4.93 us (2%)
    psum x1, blocking collectives, on_device(): lax.psum((query_part, key_part, value_part, out_part, spd_part, degree_pa...  127 us
    all_to_all x1, blocking collectives, on_device(): lax.all_to_all(send_back.reshape(peer_count, capacity, feature_dim).astyp...  35.3 us
    all_to_all x1, waiting for transfers between devices, on_device(): lax.all_to_all(embed_table[safe_rows].reshape(peer_count, capacity, featu...  21.5 us
    all_to_all x1, blocking collectives, on_device(): lax.all_to_all(requests.reshape(peer_count, capacity), 'batch', split_axi...  20.9 us
    unnamed x42, local copies, waits for them, and re-layouts  7.15 us
    scatter-add x1, other arithmetic, on_device(): jnp.zeros((row_count, feature_dim), jnp.float32).at[target_rows]  6.64 us
  transfers between devices with their start and end apart: 3, of which 2 were waited for; matrix products, arithmetic and copies ran while one was open for 14% of the time, Pallas kernels for 0%

commit v1 on v0

--- a/solution.py
+++ b/solution.py
@@ -161,9 +161,10 @@
     table_grad = lax.psum_scatter(
         accum.astype(jnp.bfloat16), ("node", "replica"), scatter_dimension=1, tiled=True
     ).astype(jnp.float32)
-    summed = lax.psum(
-        (query_part, key_part, value_part, out_part, spd_part, degree_part), ("batch", "replica")
-    )
+    one_axis = lax.psum(
+        (query_part, key_part, value_part, out_part, spd_part, degree_part), "batch"
+    )
+    summed = lax.psum(one_axis, "replica")
     copies = float(peer_count * lax.axis_size("replica"))
     return (
         table_grad,

time: 311 us -> 372 us (1.20)
  waiting for transfers between devices: 27.2 us -> 131 us
  blocking collectives: 184 us -> 139 us
    psum x1, waiting for transfers between devices: 5.65 us -> 110 us  [on_device(): lax.psum((query_part, key_part, value_part, out_part, spd_part, degree_pa...]
    psum x1, blocking collectives: 127 us -> 72.5 us  [on_device(): lax.psum((query_part, key_part, value_part, out_part, spd_part, degree_pa...]
    all_to_all x1, blocking collectives: 35.3 us -> 43.3 us  [on_device(): lax.all_to_all(send_back.reshape(peer_count, capacity, feature_dim).astyp...]
  transfers between devices with their start and end apart: 3 -> 4, of which waited for: 2 -> 2; matrix products, arithmetic and copies ran while one was open for 14% -> 11% of each run, Pallas kernels for 0% -> 0%
where the time goes in v1:
time: 372 us; the launch traced here: 369 us
  blocking collectives  139 us (37%)
  waiting for transfers between devices  131 us (35%)
  other arithmetic  29.3 us (8%)
  matrix products  26.5 us (7%)
  local copies, waits for them, and re-layouts  21.6 us (6%)
  between operations  16.5 us (4%)
  starting transfers between devices  4.97 us (1%)
    psum x1, waiting for transfers between devices, on_device(): lax.psum((query_part, key_part, value_part, out_part, spd_part, degree_pa...  110 us
    psum x1, blocking collectives, on_device(): lax.psum((query_part, key_part, value_part, out_part, spd_part, degree_pa...  72.5 us
    all_to_all x1, blocking collectives, on_device(): lax.all_to_all(send_back.reshape(peer_count, capacity, feature_dim).astyp...  43.3 us
    all_to_all x1, waiting for transfers between devices, on_device(): lax.all_to_all(embed_table[safe_rows].reshape(peer_count, capacity, featu...  21.6 us
    all_to_all x1, blocking collectives, on_device(): lax.all_to_all(requests.reshape(peer_count, capacity), 'batch', split_axi...  20.9 us
  transfers between devices with their start and end apart: 4, of which 2 were waited for; matrix products, arithmetic and copies ran while one was open for 11% of the time, Pallas kernels for 0%

profile of v1, /device:TPU:8, one launch (start us, length us, event | category | flops | bytes accessed | tf_op | source)
XLA Modules:
  0.0 369.5 jit_solution(15018562542032013902)
XLA Ops:
  8.0 0.8 fusion.50
  8.8 0.6 reduce-window.6
  9.4 0.2 slice_reduce_fusion
  9.7 0.8 fusion.49
  10.4 0.7 compare_select_fusion.4
  11.1 1.6 scatter_custom_fusion
  12.8 20.9 %all_to_all.19 = s32[32,1,12]{2,1,0:T(1,128)S(1)} all-to-all(s32[32,1,12]{2,1,0:T(1,128)S(1)} %bitcast.120), channel_id=1, replica_groups=mesh['batch'=32,'node'=4,'replica'=2] {'batch'}, dimensions={0} | all-to-all | bytes 3072 | tf_op jit(solution)/shard_map/all_to_all | solution.py:48
  33.7 0.5 broadcast.245
  34.2 0.7 reduce.17
  35.0 0.6 fusion.53
  35.6 2.1 gather_fusion
  37.7 1.1 reshape.327
  38.9 4.7 %all-to-all-start.1 = ((bf16[32,12,1024]{2,1,0:T(8,128)(2,1)}), bf16[32,12,1024]{2,1,0:T(8,128)(2,1)}, u32[]{:S(2)}, u32[]{:S(2)}) async-start(bf16[32,12,1024]{2,1,0:T(8,128)(2,1)} %reshape.327), calls=%async_computation.1 | async-start | bytes 2097152 | tf_op jit(solution)/shard_map/all_to_all | solution.py:54
  43.6 1.3 fusion.2
  44.9 1.4 copy.39
  47.0 0.2 convolution_bitcast_fusion
  47.2 2.3 convolution_convert_fusion.3
  49.5 21.6 %all-to-all-done.1 = bf16[32,12,1024]{2,1,0:T(8,128)(2,1)} async-done(((bf16[32,12,1024]{2,1,0:T(8,128)(2,1)}), bf16[32,12,1024]{2,1,0:T(8,128)(2,1)}, u32[]{:S(2)}, u32[]{:S(2)}) %all-to-all-start.1) | async-done | bytes 786464 | tf_op jit(solution)/shard_map/all_to_all | solution.py:54
  71.1 1.3 reshape.328
  72.4 1.2 gather_fusion.1
  73.6 0.1 convert_reduce_fusion
  73.7 0.3 fusion.26
  74.0 1.5 convolution_convert_fusion.5
  75.5 0.5 convolution_convert_fusion.4
  76.0 0.4 fusion.11
  76.4 0.8 fusion.67
  77.2 0.5 convolution_convert_fusion.2
  77.7 0.4 multiply_reduce_fusion
  78.1 0.2 fusion.66
  78.3 0.2 fusion.17
  78.5 0.8 copy-done.1
  79.3 0.3 fusion.18
  79.6 2.1 convolution_convert_fusion.1
  81.7 2.8 convolution_convert_fusion
  84.5 1.4 fusion.60
  85.9 1.5 fusion.58
  87.4 1.4 fusion.56
  88.8 1.3 fusion.31
  90.2 0.2 reduce-scatter.4.cloned.1.call-start
  90.5 1.4 fusion.68
  91.9 1.4 convolution_add_fusion.1
  93.3 1.4 fusion.65
  94.8 3.8 %scatter_custom_fusion.1 = f32[384,1024]{1,0:T(8,128)} fusion(s32[256]{0:T(256)} %bitcast.125, bf16[256,1024]{1,0:T(8,128)(2,1)S(1)} %gather_fusion.1, f32[256,1024]{1,0:T(8,128)} %get-tuple-element.29, f32[]{:T(128)} %constant.15.clone.1, f32[256]{0:T(256)S(1)} %get-tuple-element.30, f32[256]{0:T(256)S(1)} %get-tuple-element.31, ...), kind=kCustom, calls=%fused_computation.44 | custom fusion | flops 2883584 | bytes 3674884 | tf_op jit(solution)/shard_map/scatter | solution.py:145
  98.5 2.4 convert_element_type.111
  100.9 1.2 convert_element_type.112
  102.2 43.3 %all_to_all.20 = bf16[32,12,1024]{2,1,0:T(8,128)(2,1)} all-to-all(bf16[32,12,1024]{2,1,0:T(8,128)(2,1)S(1)} %convert_element_type.112), channel_id=1, replica_groups=mesh['batch'=32,'node'=4,'replica'=2] {'batch'}, dimensions={0} | all-to-all | bytes 1572864 | tf_op jit(solution)/shard_map/all_to_all | solution.py:148
  145.5 2.4 reshape.377
  147.9 6.7 %scatter_custom_fusion.2 = f32[1024,1024]{1,0:T(8,128)} fusion(s32[384]{0:T(512)} %get-tuple-element.10, f32[384,1024]{1,0:T(8,128)} %reshape.377, f32[]{:T(128)} %constant.15.clone.1), kind=kCustom, calls=%fused_computation.11 | custom fusion | flops 393216 | bytes 4194816 | tf_op jit(solution)/shard_map/scatter-add | solution.py:159
  154.5 3.8 %convert_element_type.113 = bf16[1024,1024]{1,0:T(8,128)(2,1)} convert(f32[1024,1024]{1,0:T(8,128)} %scatter_custom_fusion.2) | non-fusion elementwise | flops 1048576 | bytes 6291456 | tf_op jit(solution)/shard_map/convert_element_type | solution.py:162
  158.4 4.0 %copy.52 = bf16[1024,1024]{0,1:T(8,128)(2,1)} copy(bf16[1024,1024]{1,0:T(8,128)(2,1)} %convert_element_type.113) | data formatting | bytes 4194304
  162.4 109.8 %all-reduce.7.cloned.1.call-done = (f32[1024,256]{1,0:T(8,128)}, f32[1024,256]{1,0:T(8,128)}, f32[1024,256]{1,0:T(8,128)}, f32[256,1024]{1,0:T(8,128)}) async-done(((f32[1024,256]{1,0:T(8,128)}, f32[1024,256]{1,0:T(8,128)}, f32[1024,256]{1,0:T(8,128)}, f32[256,1024]{1,0:T(8,128)}), (f32[1024,256]{1,0:T(8,128)}, f32[1024,256]{1,0:T(8,128)}, f32[1024,256]{1,0:T(8,128)}, ...) | async-done | bytes 4194320 | tf_op jit(solution)/shard_map/psum | solution.py:164
  272.3 1.2 copy-done.2
  273.5 1.3 copy.46
  274.8 3.9 %fusion.19 = f32[16,4]{0,1:T(4,128)S(1)} fusion(f32[4,256,256]{2,0,1:T(4,128)} %copy.46, s32[256,256]{1,0:T(8,128)S(1)} %bitcast.117), kind=kOutput, calls=%fused_computation.39 | convolution fusion | flops 51380224 | bytes 1310976 | tf_op jit(solution)/shard_map/gijb,ghij->bh/dot_general | solution.py:111
  278.7 0.2 fusion.44
  279.0 72.5 %all-reduce = (f32[16,4]{0,1:T(4,128)S(1)}, f32[32,4]{0,1:T(4,128)S(1)}) all-reduce(f32[16,4]{0,1:T(4,128)S(1)} %fusion.19, f32[32,4]{0,1:T(4,128)S(1)} %fusion.44), channel_id=1, replica_groups=mesh['batch'=32,'node'=4,'replica'=2] {'batch'}, use_global_device_ids=true, to_apply=%region_22.23 | all-reduce | flops 192 | bytes 1536 | tf_op jit(solution)/shard_map/psum | solution.py:164
  351.5 2.5 all-reduce.2
  353.9 0.6 broadcast_multiply_fusion.5
  354.5 0.6 broadcast_multiply_fusion.4
  355.1 1.1 copy.53
  356.2 0.8 convert_element_type.114
  357.1 2.4 broadcast_multiply_fusion.3
  359.5 1.1 broadcast_multiply_fusion
  360.6 1.5 broadcast_multiply_fusion.1
  (61 shorter events, 0.6 us)
Async XLA Ops:
  8.0 27.6 %copy-start = (bf16[1024,1024]{1,0:T(8,128)(2,1)S(1)}, bf16[1024,1024]{1,0:T(8,128)(2,1)}, u32[]{:S(2)}) copy-start(bf16[1024,1024]{1,0:T(8,128)(2,1)} %param.13) | copy-start | bytes 6291460
  11.1 35.8 %copy-start.15 = (s32[256,1]{0,1:T(1,128)}, s32[256,1]{0,1:T(1,128)S(1)}, u32[]{:S(2)}) copy-start(s32[256,1]{0,1:T(1,128)S(1)} %compare_select_fusion.4) | copy-start | bytes 3076
  37.7 5.9 %copy-start.12 = (s32[1,256,256]{2,1,0:T(8,128)S(1)}, s32[1,256,256]{2,1,0:T(8,128)}, u32[]{:S(2)}) copy-start(s32[1,256,256]{2,1,0:T(8,128)} %param.17) | copy-start | bytes 786436
  37.7 5.9 %copy-start.16 = (f32[16,4]{0,1:T(4,128)S(1)}, f32[16,4]{0,1:T(4,128)}, u32[]{:S(2)}) copy-start(f32[16,4]{0,1:T(4,128)} %param.23) | copy-start | bytes 772
  38.9 32.2 %all-to-all-start.1 = ((bf16[32,12,1024]{2,1,0:T(8,128)(2,1)}), bf16[32,12,1024]{2,1,0:T(8,128)(2,1)}, u32[]{:S(2)}, u32[]{:S(2)}) async-start(bf16[32,12,1024]{2,1,0:T(8,128)(2,1)} %reshape.327), calls=%async_computation.1 | async-start | bytes 2097152 | tf_op jit(solution)/shard_map/all_to_all | solution.py:54
  43.5 3.4 copy-start.17
  43.5 3.4 copy-start.18
  43.5 228.7 %all-reduce.7.cloned.1.call-start = ((), (), s32[]{:S(2)}) async-start(), calls=%async_computation.5 | async-start | bytes 8388608 | tf_op jit(solution)/shard_map/psum | solution.py:164
  73.6 2.0 copy-start.11
  73.6 2.4 copy-start.3
  76.0 1.2 copy-start.9
  76.4 1.6 copy-start.4
  76.4 1.3 copy-start.20
  77.7 0.7 copy-start.21
  78.3 1.0 copy-start.1
  79.6 2.1 copy-start.22
  85.9 2.9 copy-start.5
  85.9 2.9 copy-start.14
  90.2 264.9 %reduce-scatter.4.cloned.1.call-start = ((), (), s32[]{:S(2)}) async-start(), calls=%async_computation.4 | async-start | bytes 2359296
  90.5 2.9 copy-start.10
  162.4 194.7 %all-reduce.9.cloned.1.call-start = ((), (), s32[]{:S(2)}) async-start(), calls=%async_computation.6 | async-start | bytes 8388608 | tf_op jit(solution)/shard_map/psum | solution.py:167
  272.2 1.2 copy-start.2
  273.5 1.3 copy-start.13
  273.5 5.3 %copy-start.19 = (s32[1,256]{1,0:T(1,128)S(1)}, s32[1,256]{1,0:T(1,128)}, u32[]{:S(2)}) copy-start(s32[1,256]{1,0:T(1,128)} %param.18) | copy-start | bytes 3076
  357.1 2.4 copy-start.6
  357.1 3.5 copy-start.7
  357.1 3.5 copy-start.8
Sparse Core Ops, SparseCore 0:
  90.3 181.8 all-reduce.6
  275.5 36.7 all-reduce.8
Sparse Core Ops, SparseCore 1:
  162.4 31.5 reduce-scatter.3
